TPU v7x, 256 devices: a whole 4x4x8 slice. The times are simulated.
256 devices in a mesh: dp: 32 (over z, y_lo, core), seq: 8 (over y_hi, x).
Axes of the slice: x: 4, y: 4 (y_hi: 2, y_lo: 2; y = y_hi * 2 + y_lo), z: 8, core: 2. Of those that a mesh axis runs over, the one named last changes fastest.
Arguments:
- resp_q: bfloat16 [32, 8, 256, 2048], P('dp', 'seq'), may hold values from -32 to 32
- resp_k: bfloat16 [32, 8, 256, 2048], P('dp', 'seq'), may hold values from -4 to 4
- resp_v: bfloat16 [32, 8, 256, 2048], P('dp', 'seq'), may hold values from -6 to 6
- resp_grad: bfloat16 [32, 8, 256, 2048], P('dp', 'seq'), may hold values from -192 to 192
- prompt_k: bfloat16 [32, 8, 64, 2048], P('dp', 'seq'), may hold values from -6 to 6
- prompt_v: bfloat16 [32, 8, 64, 2048], P('dp', 'seq'), may hold values from -6 to 6
- group: int32 [32], replicated, may hold values from 0 to 31, each once
- resp_len: int32 [32, 8], P('dp', 'seq'), may hold values from 128 to 256, as said below
- prompt_used: int32 [32], replicated, may hold values from 256 to 512, as said below
Outputs:
- grad_q: bfloat16 [32, 8, 256, 2048], P('dp', 'seq')
- grad_k: bfloat16 [32, 8, 256, 2048], P('dp', 'seq')
- grad_v: bfloat16 [32, 8, 256, 2048], P('dp', 'seq')
- grad_prompt_k: bfloat16 [32, 8, 64, 2048], P('dp', 'seq')
- grad_prompt_v: bfloat16 [32, 8, 64, 2048], P('dp', 'seq')
Inputs may be any that keep to these rules, and one draw needn't show every extreme that they name: group is a permutation: every prompt is named by exactly one response group. `resp_len`: multiples of 128; the largest equals 256. `prompt_used`: multiples of 64, at least half of 512; the largest equals 512.
All inputs are finite; a program needn't handle non-finite values.
Results may differ from a plain program's by a relative error of at most 0.017.
Values may be sent and summed in bfloat16 or wider, within the bound.
A program may use at most 128 MiB of HBM per device.

v0:
```python
import jax
import jax.numpy as jnp
from jax import lax
from jax.sharding import PartitionSpec as P

HEADS = 16


NEG = -1e30


def stat_update(stats, queries, masked, keys, values, valid, scale):
    top_old, total_old, weighted_old = stats
    scores = jnp.einsum("ihd,jhd->hij", queries, keys, preferred_element_type=jnp.float32) * scale
    scores = jnp.where(valid[None], scores, NEG)
    top_new = jnp.maximum(top_old, jnp.max(scores, axis=-1))
    weights = jnp.where(valid[None], jnp.exp(scores - top_new[..., None]), 0.0)
    dots = jnp.einsum("ihd,jhd->hij", masked, values, preferred_element_type=jnp.float32)
    factor = jnp.exp(top_old - top_new)
    total_new = total_old * factor + jnp.sum(weights, axis=-1)
    weighted_new = weighted_old * factor + jnp.sum(weights * dots, axis=-1)
    return (top_new, total_new, weighted_new)


def grad_update(queries, masked, keys, values, valid, lse, delta, scale):
    scores = jnp.einsum("ihd,jhd->hij", queries, keys, preferred_element_type=jnp.float32) * scale
    probs = jnp.where(valid[None], jnp.exp(scores - lse[..., None]), 0.0)
    dots = jnp.einsum("ihd,jhd->hij", masked, values, preferred_element_type=jnp.float32)
    slopes = (probs * (dots - delta[..., None])).astype(jnp.bfloat16)
    probs_low = probs.astype(jnp.bfloat16)
    grad_values = jnp.einsum("hij,ihd->jhd", probs_low, masked, preferred_element_type=jnp.float32)
    grad_keys = (
        jnp.einsum("hij,ihd->jhd", slopes, queries, preferred_element_type=jnp.float32) * scale
    )
    grad_query = (
        jnp.einsum("hij,jhd->ihd", slopes, keys, preferred_element_type=jnp.float32) * scale
    )
    return (grad_query, grad_keys, grad_values)


def on_device(resp_q, resp_k, resp_v, resp_grad, prompt_k, prompt_v, group, resp_len, prompt_used):
    rows = resp_q.shape[2]
    width = resp_q.shape[3]
    heads = HEADS
    head_size = width // heads
    scale = head_size ** (-0.5)
    count = lax.axis_size("dp")
    mine = lax.axis_index("dp")
    slots = jnp.arange(count, dtype=jnp.int32)
    chosen = jnp.sum(jnp.where(slots == mine, group, 0))
    used = jnp.sum(jnp.where(slots == chosen, prompt_used, 0))
    length = resp_len[0, 0]
    shard_rows = prompt_k.shape[2]
    piece_rows = shard_rows // count
    stacked = jnp.stack([prompt_k[0, 0], prompt_v[0, 0]], axis=0).reshape(
        2, count, piece_rows, width
    )
    spread_out = lax.all_to_all(stacked, "dp", split_axis=1, concat_axis=1, tiled=True)
    outgoing = jnp.take(spread_out, group, axis=1)
    arrived = lax.all_to_all(outgoing, "dp", split_axis=1, concat_axis=1, tiled=True)
    shard = arrived.reshape(2, count * piece_rows, width)
    plen = shard.shape[1] * lax.axis_size("seq")
    queries = resp_q[0, 0].reshape(rows, heads, head_size)
    own_keys = resp_k[0, 0].reshape(rows, heads, head_size)
    own_values = resp_v[0, 0].reshape(rows, heads, head_size)
    positions = jnp.arange(rows, dtype=jnp.int32)
    masked = jnp.where(
        (positions < length)[:, None], resp_grad[0, 0], jnp.zeros_like(resp_grad[0, 0])
    )
    masked = masked.reshape(rows, heads, head_size)
    self_valid = (positions[None, :] <= positions[:, None]) & (positions[None, :] < length)
    stats = (
        jnp.full((heads, rows), NEG, jnp.float32),
        jnp.zeros((heads, rows), jnp.float32),
        jnp.zeros((heads, rows), jnp.float32),
    )
    whole = lax.all_gather(shard, "seq", axis=1, tiled=True)
    stats_stats = stats
    total_rows = whole.shape[1]
    step = total_rows
    first = 0
    keys = whole[0, first : first + step].reshape(step, heads, head_size)
    values = whole[1, first : first + step].reshape(step, heads, head_size)
    index = 0 + first + jnp.arange(step, dtype=jnp.int32)
    valid = jnp.broadcast_to((index < used)[None, :], (rows, step))
    stats_stats = stat_update(stats_stats, queries, masked, keys, values, valid, scale)
    stats = stats_stats
    stats = stat_update(stats, queries, masked, own_keys, own_values, self_valid, scale)
    top, total, weighted = stats
    lse = top + jnp.log(total)
    delta = weighted / total
    carry = (
        jnp.zeros((rows, heads, head_size), jnp.float32),
        jnp.zeros((2, plen, width), jnp.float32),
    )
    total_rows = whole.shape[1]
    step = total_rows
    first = 0
    keys = whole[0, first : first + step].reshape(step, heads, head_size)
    values = whole[1, first : first + step].reshape(step, heads, head_size)
    index = 0 + first + jnp.arange(step, dtype=jnp.int32)
    valid = jnp.broadcast_to((index < used)[None, :], (rows, step))
    query_term, key_term, value_term = grad_update(
        queries, masked, keys, values, valid, lse, delta, scale
    )
    query_sum = query_term
    block = jnp.stack([key_term.reshape(step, width), value_term.reshape(step, width)], axis=0)
    block = block.astype(jnp.bfloat16).astype(jnp.float32)
    buffer = block
    carry = (query_sum, buffer)
    query_sum, buffer = carry
    query_term, key_own, value_own = grad_update(
        queries, masked, own_keys, own_values, self_valid, lse, delta, scale
    )
    query_sum = query_sum + query_term
    summed = lax.psum_scatter(buffer.astype(jnp.bfloat16), "seq", scatter_dimension=1, tiled=True)
    returned = summed.reshape(2, count, piece_rows, width)
    back = lax.all_to_all(returned, "dp", split_axis=1, concat_axis=1, tiled=True)
    owner_table = group[None, :] == slots[:, None]
    inverse = jnp.sum(jnp.where(owner_table, slots[None, :], 0), axis=1)
    ordered = jnp.take(back, inverse, axis=1)
    owned = lax.all_to_all(ordered, "dp", split_axis=1, concat_axis=1, tiled=True).reshape(
        2, shard_rows, width
    )
    grad_q = query_sum.reshape(1, 1, rows, width).astype(jnp.bfloat16)
    grad_k = key_own.reshape(1, 1, rows, width).astype(jnp.bfloat16)
    grad_v = value_own.reshape(1, 1, rows, width).astype(jnp.bfloat16)
    grad_prompt_k = owned[0].reshape(1, 1, shard_rows, width)
    grad_prompt_v = owned[1].reshape(1, 1, shard_rows, width)
    return (grad_q, grad_k, grad_v, grad_prompt_k, grad_prompt_v)


def solution(mesh):
    in_specs = (
        P("dp", "seq", None, None),
        P("dp", "seq", None, None),
        P("dp", "seq", None, None),
        P("dp", "seq", None, None),
        P("dp", "seq", None, None),
        P("dp", "seq", None, None),
        P(),
        P("dp", "seq"),
        P(),
    )
    out_specs = (
        P("dp", "seq", None, None),
        P("dp", "seq", None, None),
        P("dp", "seq", None, None),
        P("dp", "seq", None, None),
        P("dp", "seq", None, None),
    )
    return jax.shard_map(
        on_device, mesh=mesh, in_specs=in_specs, out_specs=out_specs, check_vma=False
    )
```

profile of v0, /device:TPU:1, one launch (start us, length us, event | category | flops | bytes accessed | tf_op | source)
XLA Modules:
  0.0 398.2 jit_solution(6901603739111923657)
XLA Ops:
  7.2 1.1 stack.12
  8.3 1.2 stack.11
  9.5 1.5 pad_maximum_fusion.1
  11.0 11.1 %all-to-all-start = ((bf16[2,32,2,2048]{3,2,0,1:T(2,128)(2,1)}), bf16[2,32,2,2048]{3,2,0,1:T(2,128)(2,1)S(1)}, u32[]{:S(2)}, u32[]{:S(2)}) async-start(bf16[2,32,2,2048]{3,2,0,1:T(2,128)(2,1)} %pad_maximum_fusion.1), calls=%async_computation | async-start | bytes 1048576 | tf_op jit(solution)/shard_map/all_to_all | solution.py:58
  22.2 1.3 fusion.32
  23.5 0.7 compare_and_fusion.1
  24.2 14.7 %all-to-all-done = bf16[2,32,2,2048]{3,2,0,1:T(2,128)(2,1)S(1)} async-done(((bf16[2,32,2,2048]{3,2,0,1:T(2,128)(2,1)}), bf16[2,32,2,2048]{3,2,0,1:T(2,128)(2,1)S(1)}, u32[]{:S(2)}, u32[]{:S(2)}) %all-to-all-start) | async-done | bytes 524320 | tf_op jit(solution)/shard_map/all_to_all | solution.py:58
  39.2 1.6 gather_fusion
  41.4 21.2 %all_to_all.20 = bf16[2,32,2,2048]{3,2,0,1:T(2,128)(2,1)S(1)} all-to-all(bf16[2,32,2,2048]{3,2,0,1:T(2,128)(2,1)S(1)} %fusion.29), channel_id=1, replica_groups=mesh['dp'=32,'seq'=8] {'dp'}, dimensions={1} | all-to-all | bytes 1048576 | tf_op jit(solution)/shard_map/all_to_all | solution.py:60
  62.7 1.3 copy.124
  65.5 1.5 copy.167
  66.9 2.3 copy.164
  69.2 2.4 copy.169
  71.7 1.3 fusion.33
  73.7 2.8 select_reduce_fusion
  76.6 61.1 %all-gather.2.cloned.1.call-done = bf16[2,512,2048]{2,0,1:T(2,128)(2,1)} async-done(((bf16[2,64,2048]{2,0,1:T(2,128)(2,1)}), bf16[2,512,2048]{2,0,1:T(2,128)(2,1)}) %all-gather.2.cloned.1.call-update) | async-done | bytes 4194320 | tf_op jit(solution)/shard_map/all_gather | solution.py:77
  137.7 9.9 %fusion.43 = (bf16[1,512,2048]{2,0,1:T(2,128)(2,1)}, bf16[1,512,2048]{2,0,1:T(2,128)(2,1)}) fusion(bf16[2,512,2048]{2,0,1:T(2,128)(2,1)} %all-gather.2.cloned.1.call-done), kind=kLoop, calls=%fused_computation.81 | loop fusion | bytes 8388608 | tf_op jit(solution)/shard_map/slice | solution.py:100
  147.6 9.0 %copy.165 = bf16[1,512,2048]{1,2,0:T(8,128)(2,1)S(1)} copy(bf16[1,512,2048]{2,0,1:T(2,128)(2,1)} %get-tuple-element.36) | data formatting | bytes 4194304
  156.6 10.8 %copy.166 = bf16[1,512,2048]{1,2,0:T(8,128)(2,1)} copy(bf16[1,512,2048]{2,0,1:T(2,128)(2,1)} %get-tuple-element.35) | data formatting | bytes 4194304
  167.3 2.2 bitcast_reduce_fusion
  170.1 3.5 fusion.10
  173.6 6.0 %fusion.3 = (f32[16,256]{1,0:T(8,128)S(1)}, f32[16,256]{1,0:T(8,128)S(1)}, f32[16,256,512]{1,2,0:T(8,128)}) fusion(f32[16,512,256]{2,1,0:T(8,128)S(1)} %get-tuple-element.46, f32[16,256]{1,0:T(8,128)S(1)} %get-tuple-element.41, pred[512]{0:T(512)(128)(4,1)S(1)} %iota_compare_fusion.2, bf16[512,16,128]{0,2,1:T(8,128)(2,1)S(1)} %bitcast.88, ...), kind=kOutput, calls=%fused_computation.11 | convolution fusion | flops 552067072 | bytes 19972864 | tf_op jit(solution)/shard_map/ihd,jhd->hij/dot_general | solution.py:28
  179.7 2.1 fusion.18
  181.7 7.8 %copy.148 = bf16[1,512,2048]{2,0,1:T(2,128)(2,1)} copy(bf16[1,512,2048]{1,2,0:T(8,128)(2,1)S(1)} %bitcast.89) | data formatting | bytes 4194304 | tf_op jit(solution)/shard_map/stack;reshape | solution.py:107
  189.5 7.3 %fusion = bf16[16,256,512]{1,2,0:T(8,128)(2,1)S(1)} fusion(f32[16,256,512]{1,2,0:T(8,128)} %get-tuple-element.50, f32[16,512,256]{2,1,0:T(8,128)} %copy-done.1, f32[16,256]{1,0:T(8,128)S(1)} %get-tuple-element.40, f32[16,256]{1,0:T(8,128)S(1)} %get-tuple-element.39, pred[512]{0:T(512)(128)(4,1)S(1)} %iota_compare_fusion.2), kind=kLoop, calls=%fused_computation.4 | loop fusion | flops 12582912 | bytes 21004800 | tf_op jit(solution)/shard_map/convert_element_type | solution.py:29
  196.8 1.9 copy-done
  198.7 1.5 multiply_convert_fusion
  200.3 7.8 %copy.147 = bf16[1,512,2048]{2,0,1:T(2,128)(2,1)} copy(bf16[1,512,2048]{1,2,0:T(8,128)(2,1)S(1)} %bitcast.85) | data formatting | bytes 4194304 | tf_op jit(solution)/shard_map/stack;reshape | solution.py:107
  208.0 10.9 %pad_maximum_fusion = bf16[2,512,2048]{2,0,1:T(2,128)(2,1)} fusion(bf16[1,512,2048]{2,0,1:T(2,128)(2,1)} %copy.148, bf16[1,512,2048]{2,0,1:T(2,128)(2,1)} %copy.147), kind=kLoop, calls=%fused_computation.13 | loop fusion | flops 8388608 | bytes 8388608 | tf_op jit(solution)/shard_map/stack | solution.py:107
  221.0 111.3 %all-reduce.3.cloned.1.call-done = bf16[2,512,2048]{2,0,1:T(2,128)(2,1)} async-done(((bf16[2,512,2048]{2,0,1:T(2,128)(2,1)}), bf16[2,512,2048]{2,0,1:T(2,128)(2,1)}) %all-reduce.3.cloned.1.call-update) | async-done | bytes 4194320
  332.3 1.4 constant_dynamic-slice_fusion
  333.7 1.3 copy.149
  335.0 7.9 %all-to-all-start.2 = ((bf16[2,32,2,2048]{3,2,0,1:T(2,128)(2,1)}), bf16[2,32,2,2048]{3,2,0,1:T(2,128)(2,1)}, u32[]{:S(2)}, u32[]{:S(2)}) async-start(bf16[2,32,2,2048]{3,2,0,1:T(2,128)(2,1)} %copy.149), calls=%async_computation.2 | async-start | bytes 1048576 | tf_op jit(solution)/shard_map/all_to_all | solution.py:118
  343.0 4.6 %multiply_convert_fusion.1 = bf16[16,256,256]{1,2,0:T(8,128)(2,1)S(1)} fusion(f32[16,256,256]{1,2,0:T(8,128)} %get-tuple-element.49, f32[16,256,256]{1,2,0:T(8,128)} %get-tuple-element.48, f32[16,256]{1,0:T(8,128)S(1)} %get-tuple-element.40, f32[16,256]{1,0:T(8,128)S(1)} %get-tuple-element.39, pred[256,256]{0,1:T(8,128)(4,1)S(1)} %fusion.31), kind=kLoop, calls=%fused_computation.15 | loop fusion | flops 6291456 | bytes 10584064 | tf_op jit(solution)/shard_map/convert_element_type | solution.py:29
  347.6 1.8 fusion.45
  349.4 10.3 %all-to-all-done.2 = bf16[2,32,2,2048]{3,2,0,1:T(2,128)(2,1)} async-done(((bf16[2,32,2,2048]{3,2,0,1:T(2,128)(2,1)}), bf16[2,32,2,2048]{3,2,0,1:T(2,128)(2,1)}, u32[]{:S(2)}, u32[]{:S(2)}) %all-to-all-start.2) | async-done | bytes 524320 | tf_op jit(solution)/shard_map/all_to_all | solution.py:118
  359.7 3.4 gather_fusion.1
  363.1 2.4 fusion.30
  365.5 5.7 %all-to-all-start.3 = ((bf16[2,32,2,2048]{3,2,0,1:T(2,128)(2,1)}), bf16[2,32,2,2048]{3,2,0,1:T(2,128)(2,1)}, u32[]{:S(2)}, u32[]{:S(2)}) async-start(bf16[2,32,2,2048]{3,2,0,1:T(2,128)(2,1)} %fusion.30), calls=%async_computation.3 | async-start | bytes 1048576 | tf_op jit(solution)/shard_map/all_to_all | solution.py:122
  371.3 5.2 %fusion.13 = bf16[256,16,128]{0,2,1:T(8,128)(2,1)} fusion(f32[16,256,128]{1,2,0:T(8,128)} %fusion.45, bf16[512,16,128]{0,2,1:T(8,128)(2,1)} %bitcast.82, bf16[16,256,512]{1,2,0:T(8,128)(2,1)} %copy-done), kind=kOutput, calls=%fused_computation.28 | convolution fusion | flops 538968064 | bytes 9437184 | tf_op jit(solution)/shard_map/hij,jhd->ihd/dot_general | solution.py:36
  376.5 2.3 copy.150
  378.8 1.8 multiply_convert_fusion.2
  380.5 2.3 copy.151
  382.8 3.5 fusion.19
  386.3 1.4 copy.152
  388.4 1.4 fusion.44
  389.8 0.8 reshape_squeeze.28
  390.6 0.8 reshape_squeeze.29
  (44 shorter events, 5.2 us)
Async XLA Ops:
  8.3 56.0 %copy-start.7 = (bf16[1,1,256,2048]{3,2,1,0:T(8,128)(2,1)S(1)}, bf16[1,1,256,2048]{3,2,1,0:T(8,128)(2,1)}, u32[]{:S(2)}) copy-start(bf16[1,1,256,2048]{3,2,1,0:T(8,128)(2,1)} %param.12) | copy-start | bytes 3145732
  11.0 27.9 %all-to-all-start = ((bf16[2,32,2,2048]{3,2,0,1:T(2,128)(2,1)}), bf16[2,32,2,2048]{3,2,0,1:T(2,128)(2,1)S(1)}, u32[]{:S(2)}, u32[]{:S(2)}) async-start(bf16[2,32,2,2048]{3,2,0,1:T(2,128)(2,1)} %pad_maximum_fusion.1), calls=%async_computation | async-start | bytes 1048576 | tf_op jit(solution)/shard_map/all_to_all | solution.py:58
  22.2 115.5 %all-gather.2.cloned.1.call-start = ((), (), s32[]{:S(2)}) async-start(), calls=%async_computation.4 | async-start | bytes 4718592 | tf_op jit(solution)/shard_map/all_gather | solution.py:77
  64.0 7.7 %copy-start.11 = (s32[32]{0:T(128)S(1)}, s32[32]{0:T(128)}, u32[]{:S(2)}) copy-start(s32[32]{0:T(128)} %param.19) | copy-start | bytes 388
  64.0 268.2 %all-reduce.3.cloned.1.call-start = ((), (), s32[]{:S(2)}) async-start(), calls=%async_computation.5 | async-start | bytes 8388608
  64.8 11.8 %copy-start.4 = (bf16[1,1,256,2048]{2,3,1,0:T(8,128)(2,1)}, bf16[1,1,256,2048]{2,3,1,0:T(8,128)(2,1)S(1)}, u32[]{:S(2)}) copy-start(bf16[1,1,256,2048]{2,3,1,0:T(8,128)(2,1)S(1)} %copy.168) | copy-start | bytes 3145732
  156.6 12.9 %copy-start.2 = (bf16[1,512,2048]{1,2,0:T(8,128)(2,1)}, bf16[1,512,2048]{1,2,0:T(8,128)(2,1)S(1)}, u32[]{:S(2)}) copy-start(bf16[1,512,2048]{1,2,0:T(8,128)(2,1)S(1)} %copy.165) | copy-start | bytes 6291460
  167.3 2.2 copy-start.3
  167.3 2.5 copy-start.8
  167.3 2.8 copy-start.9
  169.5 10.2 %copy-start.1 = (f32[16,512,256]{2,1,0:T(8,128)}, f32[16,512,256]{2,1,0:T(8,128)S(1)}, u32[]{:S(2)}) copy-start(f32[16,512,256]{2,1,0:T(8,128)S(1)} %get-tuple-element.46) | copy-start | bytes 25165828
  170.1 3.5 copy-start.6
  196.8 1.9 copy-start
  218.9 0.7 copy-start.12
  218.9 1.9 copy-start.10
  335.0 24.7 %all-to-all-start.2 = ((bf16[2,32,2,2048]{3,2,0,1:T(2,128)(2,1)}), bf16[2,32,2,2048]{3,2,0,1:T(2,128)(2,1)}, u32[]{:S(2)}, u32[]{:S(2)}) async-start(bf16[2,32,2,2048]{3,2,0,1:T(2,128)(2,1)} %copy.149), calls=%async_computation.2 | async-start | bytes 1048576 | tf_op jit(solution)/shard_map/all_to_all | solution.py:118
  343.0 4.7 %copy-start.5 = (bf16[1,1,256,2048]{2,3,1,0:T(8,128)(2,1)S(1)}, bf16[1,1,256,2048]{2,3,1,0:T(8,128)(2,1)}, u32[]{:S(2)}) copy-start(bf16[1,1,256,2048]{2,3,1,0:T(8,128)(2,1)} %copy-done.4) | copy-start | bytes 3145732
  365.5 22.9 %all-to-all-start.3 = ((bf16[2,32,2,2048]{3,2,0,1:T(2,128)(2,1)}), bf16[2,32,2,2048]{3,2,0,1:T(2,128)(2,1)}, u32[]{:S(2)}, u32[]{:S(2)}) async-start(bf16[2,32,2,2048]{3,2,0,1:T(2,128)(2,1)} %fusion.30), calls=%async_computation.3 | async-start | bytes 1048576 | tf_op jit(solution)/shard_map/all_to_all | solution.py:122
Sparse Core Ops, SparseCore 0:
  64.1 73.4 all-gather.1
  219.1 113.1 all-reduce.2
where the time goes:
time: 399 us; the launch traced here: 398 us
  waiting for transfers between devices  198 us (50%)
  local copies, waits for them, and re-layouts  76.4 us (19%)
  other arithmetic  31.5 us (8%)
  matrix products  30.4 us (8%)
  starting transfers between devices  25.1 us (6%)
  blocking collectives  21.2 us (5%)
  between operations  15.6 us (4%)
    unnamed x3, waiting for transfers between devices  111 us
    all_gather x1, waiting for transfers between devices, on_device(): whole = lax.all_gather(shard, 'seq', axis=1, tiled=True)  61.1 us
    unnamed x34, local copies, waits for them, and re-layouts  33.3 us
    all_to_all x1, blocking collectives, on_device(): lax.all_to_all(outgoing, 'dp', split_axis=1, concat_axis=1, tiled=True)  21.2 us
    another operation x2, local copies, waits for them, and re-layouts, on_device(): jnp.stack([key_term.reshape(step, width), value_term.reshape(step, width)...  15.5 us
    all_to_all x1, waiting for transfers between devices, on_device(): lax.all_to_all(stacked, 'dp', split_axis=1, concat_axis=1, tiled=True)  14.7 us
    convert_element_type x2, other arithmetic, grad_update(): slopes = (probs * (dots - delta[..., None])).astype(jnp.bfloat16)  11.9 us
    all_to_all x1, starting transfers between devices, on_device(): lax.all_to_all(stacked, 'dp', split_axis=1, concat_axis=1, tiled=True)  11.1 us
  transfers between devices with their start and end apart: 5, of which 5 were waited for; matrix products, arithmetic and copies ran while one was open for 9% of the time, Pallas kernels for 0%

commit v1 on v0

v1 whole, which is shorter than its diff:
```python
import functools

import jax
import jax.numpy as jnp
from jax import lax
from jax.experimental import pallas as pl
from jax.experimental.pallas import tpu as pltpu
from jax.sharding import PartitionSpec as P

HEADS = 16
NEG = -1e30
LOG2E = 1.4426950408889634
NT = (((1,), (1,)), ((), ()))
TN = (((0,), (0,)), ((), ()))
NN = (((1,), (0,)), ((), ()))


def dot(a, b, dims):
    return lax.dot_general(a, b, dims, preferred_element_type=jnp.float32)


def head_grads(q, g, kp, ko, vp, vo, bias_p, bias_o, scale):
    c = scale * LOG2E
    sp = dot(kp, q, NT) * c + bias_p
    so = dot(ko, q, NT) * c + bias_o
    top = jnp.maximum(jnp.max(sp, 0, keepdims=True), jnp.max(so, 0, keepdims=True))
    pp = jnp.exp2(sp - top)
    po = jnp.exp2(so - top)
    inv = 1.0 / (jnp.sum(pp, 0, keepdims=True) + jnp.sum(po, 0, keepdims=True))
    dp = dot(vp, g, NT)
    do = dot(vo, g, NT)
    delta = (jnp.sum(pp * dp, 0, keepdims=True) + jnp.sum(po * do, 0, keepdims=True)) * inv
    pp = pp * inv
    po = po * inv
    lp = pp.astype(jnp.bfloat16)
    lo = po.astype(jnp.bfloat16)
    tp = (pp * (dp - delta)).astype(jnp.bfloat16)
    to = (po * (do - delta)).astype(jnp.bfloat16)
    gq = (dot(tp, kp, TN) + dot(to, ko, TN)) * scale
    gko = dot(to, q, NN) * scale
    gvo = dot(lo, g, NN)
    gkp = dot(tp, q, NN) * scale
    gvp = dot(lp, g, NN)
    return tuple(x.astype(jnp.bfloat16) for x in (gq, gko, gvo, gkp, gvp))


def grads_kernel(step, scale, used, length, q, k, v, g, kp, vp, gq, gk, gv, pk, pv):
    rows, plen = q.shape[0], kp.shape[0]
    bias_p = jnp.where(lax.broadcasted_iota(jnp.int32, (plen, rows), 0) < used[0], 0.0, NEG)
    key = lax.broadcasted_iota(jnp.int32, (rows, rows), 0)
    query = lax.broadcasted_iota(jnp.int32, (rows, rows), 1)
    bias_o = jnp.where((key <= query) & (key < length[0]), 0.0, NEG)
    live = lax.broadcasted_iota(jnp.int32, (rows, 128), 0) < length[0]
    for u in range(step):
        s = slice(u * 128, u * 128 + 128)
        masked = jnp.where(live, g[:, s], jnp.zeros_like(g[:, s]))
        gq[:, s], gk[:, s], gv[:, s], pk[:, s], pv[:, s] = head_grads(
            q[:, s], masked, kp[:, s], k[:, s], vp[:, s], v[:, s], bias_p, bias_o, scale
        )


def grads(q, k, v, g, kp, vp, used, length):
    rows, width = q.shape
    plen = kp.shape[0]
    step = 2
    own = pl.BlockSpec((rows, 128 * step), lambda h: (0, h))
    prompt = pl.BlockSpec((plen, 128 * step), lambda h: (0, h))
    scalar = pl.BlockSpec(memory_space=pltpu.SMEM)
    shape = lambda r: jax.ShapeDtypeStruct((r, width), jnp.bfloat16)
    return pl.pallas_call(
        functools.partial(grads_kernel, step, 128**-0.5),
        grid=(width // (128 * step),),
        in_specs=[scalar, scalar, own, own, own, own, prompt, prompt],
        out_specs=[own, own, own, prompt, prompt],
        out_shape=[shape(rows)] * 3 + [shape(plen)] * 2,
        compiler_params=pltpu.CompilerParams(vmem_limit_bytes=40 * 2**20),
    )(used, length, q, k, v, g, kp, vp)


def on_device(resp_q, resp_k, resp_v, resp_grad, prompt_k, prompt_v, group, resp_len, prompt_used):
    rows, width = resp_q.shape[2:]
    count = lax.axis_size("dp")
    mine = lax.axis_index("dp")
    slots = jnp.arange(count, dtype=jnp.int32)
    chosen = jnp.sum(jnp.where(slots == mine, group, 0))
    used = jnp.sum(jnp.where(slots == chosen, prompt_used, 0))
    shard_rows = prompt_k.shape[2]
    piece_rows = shard_rows // count
    stacked = jnp.stack([prompt_k[0, 0], prompt_v[0, 0]], axis=0).reshape(
        2, count, piece_rows, width
    )
    spread_out = lax.all_to_all(stacked, "dp", split_axis=1, concat_axis=1, tiled=True)
    outgoing = jnp.take(spread_out, group, axis=1)
    arrived = lax.all_to_all(outgoing, "dp", split_axis=1, concat_axis=1, tiled=True)
    shard = arrived.reshape(2, shard_rows, width)
    whole = lax.all_gather(shard, "seq", axis=1, tiled=True)
    grad_q, grad_k, grad_v, part_k, part_v = grads(
        resp_q[0, 0], resp_k[0, 0], resp_v[0, 0], resp_grad[0, 0],
        whole[0], whole[1], used.reshape(1), resp_len[0],
    )
    buffer = jnp.stack([part_k, part_v], axis=0)
    summed = lax.psum_scatter(buffer, "seq", scatter_dimension=1, tiled=True)
    returned = summed.reshape(2, count, piece_rows, width)
    back = lax.all_to_all(returned, "dp", split_axis=1, concat_axis=1, tiled=True)
    owner_table = group[None, :] == slots[:, None]
    inverse = jnp.sum(jnp.where(owner_table, slots[None, :], 0), axis=1)
    ordered = jnp.take(back, inverse, axis=1)
    owned = lax.all_to_all(ordered, "dp", split_axis=1, concat_axis=1, tiled=True).reshape(
        2, shard_rows, width
    )
    return (
        grad_q[None, None], grad_k[None, None], grad_v[None, None],
        owned[0][None, None], owned[1][None, None],
    )


def solution(mesh):
    split = P("dp", "seq", None, None)
    return jax.shard_map(
        on_device,
        mesh=mesh,
        in_specs=(split,) * 6 + (P(), P("dp", "seq"), P()),
        out_specs=(split,) * 5,
        check_vma=False,
    )
```

time: 399 us -> 309 us (0.77)
  local copies, waits for them, and re-layouts: 76.4 us -> 14.8 us
  matrix products: 30.4 us -> 0 us
  other arithmetic: 31.5 us -> 6.97 us
  blocking collectives: 21.2 us -> 42.5 us
  Pallas kernels: 0 us -> 18.1 us
  waiting for transfers between devices: 198 us -> 191 us
  starting transfers between devices: 25.1 us -> 20.4 us
    unnamed x3 -> x2, waiting for transfers between devices: 111 us -> 0.03 us
    reduce_scatter x0 -> x1, waiting for transfers between devices: none -> 87.1 us  [on_device(): summed = lax.psum_scatter(buffer, 'seq', scatter_dimension=1, tiled=True)]
    unnamed x34 -> x12, local copies, waits for them, and re-layouts: 33.3 us -> 0.03 us
    dot_general x10 -> x0, matrix products: 30.4 us -> none  [the longest x2 7.02 us: grad_update(): jnp.einsum('hij,jhd->ihd', slopes, keys, preferred_element_type=jnp.float32)]
    all_to_all x0 -> x1, blocking collectives: none -> 21.2 us  [on_device(): lax.all_to_all(ordered, 'dp', split_axis=1, concat_axis=1, tiled=True)]
    pallas_call x0 -> x1, Pallas kernels: none -> 18.1 us  [grads(): pl.pallas_call(functools.partial(grads_kernel, step, 128 ** (-0.5)), grid...]
    another operation x6 -> x2, local copies, waits for them, and re-layouts: 19.1 us -> 1.6 us  [the longest x1 0.8 us: on_device(): owned[0][None, None]]
    convert_element_type x2 -> x0, other arithmetic: 11.9 us -> none  [grad_update(): slopes = (probs * (dots - delta[..., None])).astype(jnp.bfloat16)]
  transfers between devices with their start and end apart: 5 -> 4, of which waited for: 5 -> 4; matrix products, arithmetic and copies ran while one was open for 9% -> 1% of each run, Pallas kernels for 0% -> 0%
where the time goes in v1:
time: 309 us
  waiting for transfers between devices  191 us (62%)
  blocking collectives  42.5 us (14%)
  starting transfers between devices  20.4 us (7%)
  Pallas kernels  18.1 us (6%)
  local copies, waits for them, and re-layouts  14.8 us (5%)
  between operations  14.8 us (5%)
  other arithmetic  6.97 us (2%)
    reduce_scatter x1, waiting for transfers between devices, on_device(): summed = lax.psum_scatter(buffer, 'seq', scatter_dimension=1, tiled=True)  87.1 us
    all_gather x1, waiting for transfers between devices, on_device(): whole = lax.all_gather(shard, 'seq', axis=1, tiled=True)  71.6 us
    all_to_all x1, blocking collectives, on_device(): lax.all_to_all(outgoing, 'dp', split_axis=1, concat_axis=1, tiled=True)  21.2 us
    all_to_all x1, blocking collectives, on_device(): lax.all_to_all(ordered, 'dp', split_axis=1, concat_axis=1, tiled=True)  21.2 us
    pallas_call x1, Pallas kernels, grads(): pl.pallas_call(functools.partial(grads_kernel, step, 128 ** (-0.5)), grid...  18.1 us
    all_to_all x1, waiting for transfers between devices, on_device(): lax.all_to_all(returned, 'dp', split_axis=1, concat_axis=1, tiled=True)  16.6 us
    all_to_all x1, waiting for transfers between devices, on_device(): lax.all_to_all(stacked, 'dp', split_axis=1, concat_axis=1, tiled=True)  16 us
    all_to_all x1, starting transfers between devices, on_device(): lax.all_to_all(stacked, 'dp', split_axis=1, concat_axis=1, tiled=True)  11.1 us
  transfers between devices with their start and end apart: 4, of which 4 were waited for; matrix products, arithmetic and copies ran while one was open for 1% of the time, Pallas kernels for 0%

profile of v1, /device:TPU:1, one launch (start us, length us, event | category | flops | bytes accessed | tf_op | source)
XLA Modules:
  0.0 308.9 jit_solution(12316512664404967996)
XLA Ops:
  7.2 0.0 copy-start.4
  7.2 1.1 stack.16
  8.3 1.1 stack.17
  9.5 1.5 pad_maximum_fusion.1
  10.9 11.1 %all-to-all-start = ((bf16[2,32,2,2048]{3,2,0,1:T(2,128)(2,1)}), bf16[2,32,2,2048]{3,2,0,1:T(2,128)(2,1)S(1)}, u32[]{:S(2)}, u32[]{:S(2)}) async-start(bf16[2,32,2,2048]{3,2,0,1:T(2,128)(2,1)} %pad_maximum_fusion.1), calls=%async_computation | async-start | bytes 1048576 | tf_op jit(solution)/shard_map/all_to_all | solution.py:92
  22.1 0.0 all-gather.2.cloned.1.call-start
  22.1 0.0 copy-done.4
  22.1 0.6 compare_select_fusion.1
  22.8 16.0 %all-to-all-done = bf16[2,32,2,2048]{3,2,0,1:T(2,128)(2,1)S(1)} async-done(((bf16[2,32,2,2048]{3,2,0,1:T(2,128)(2,1)}), bf16[2,32,2,2048]{3,2,0,1:T(2,128)(2,1)S(1)}, u32[]{:S(2)}, u32[]{:S(2)}) %all-to-all-start) | async-done | bytes 524320 | tf_op jit(solution)/shard_map/all_to_all | solution.py:92
  38.8 0.4 copy.18
  39.2 1.6 gather_fusion
  40.8 0.6 fusion
  41.3 0.0 copy-start.5
  41.4 21.2 %all_to_all.20 = bf16[2,32,2,2048]{3,2,0,1:T(2,128)(2,1)S(1)} all-to-all(bf16[2,32,2,2048]{3,2,0,1:T(2,128)(2,1)S(1)} %fusion), channel_id=1, replica_groups=mesh['dp'=32,'seq'=8] {'dp'}, dimensions={1} | all-to-all | bytes 1048576 | tf_op jit(solution)/shard_map/all_to_all | solution.py:94
  62.6 0.4 copy.19
  63.0 1.0 reshape.36
  64.0 0.0 all-gather.2.cloned.1.call-update
  64.0 0.0 reduce-scatter.2.cloned.1.call-start
  64.7 0.0 copy-done.5
  64.7 1.3 fusion.3
  66.0 0.0 copy-start
  66.0 0.0 copy-start.1
  66.0 0.0 copy-start.2
  66.0 71.6 %all-gather.2.cloned.1.call-done = bf16[2,512,2048]{2,1,0:T(8,128)(2,1)} async-done(((bf16[2,64,2048]{2,1,0:T(8,128)(2,1)}), bf16[2,512,2048]{2,1,0:T(8,128)(2,1)}) %all-gather.2.cloned.1.call-update) | async-done | bytes 4194320 | tf_op jit(solution)/shard_map/all_gather | solution.py:96
  137.6 0.0 copy-start.3
  137.6 2.9 slice_bitcast_fusion
  140.5 0.0 copy-done
  140.5 0.0 copy-done.1
  140.5 0.0 copy-done.2
  140.5 0.0 copy-done.3
  140.5 18.1 %shard_map.128 = (bf16[256,2048]{1,0:T(8,128)(2,1)}, bf16[256,2048]{1,0:T(8,128)(2,1)}, bf16[256,2048]{1,0:T(8,128)(2,1)}, bf16[512,2048]{1,0:T(8,128)(2,1)S(1)}, bf16[512,2048]{1,0:T(8,128)(2,1)S(1)}) custom-call(s32[1]{0:T(128)} %bitcast.used, s32[1]{0:T(128)} %bitcast.27.length, bf16[256,2048]{1,0:T(8,128)(2,1)S(1)} %bitcast.30, ...), custom_call_target="tpu_custom_call" | custom-call | tf_op jit(solution)/shard_map/pallas_call | solution.py:70
  158.6 2.3 pad_maximum_fusion
  160.9 0.0 reduce-scatter.2.cloned.1.call-update
  160.9 87.1 %reduce-scatter.2.cloned.1.call-done = bf16[2,64,2048]{2,1,0:T(8,128)(2,1)} async-done(((bf16[2,512,2048]{2,1,0:T(8,128)(2,1)}), bf16[2,64,2048]{2,1,0:T(8,128)(2,1)}) %reduce-scatter.2.cloned.1.call-update) | async-done | bytes 524304 | tf_op jit(solution)/shard_map/reduce_scatter | solution.py:102
  248.0 1.4 reshape.37
  249.4 1.4 copy.20
  250.7 9.2 %all-to-all-start.2 = ((bf16[2,32,2,2048]{3,2,0,1:T(2,128)(2,1)}), bf16[2,32,2,2048]{3,2,0,1:T(2,128)(2,1)S(1)}, u32[]{:S(2)}, u32[]{:S(2)}) async-start(bf16[2,32,2,2048]{3,2,0,1:T(2,128)(2,1)} %copy.20), calls=%async_computation.3 | async-start | bytes 1048576 | tf_op jit(solution)/shard_map/all_to_all | solution.py:104
  259.9 0.1 select_reduce_fusion
  260.1 16.6 %all-to-all-done.2 = bf16[2,32,2,2048]{3,2,0,1:T(2,128)(2,1)S(1)} async-done(((bf16[2,32,2,2048]{3,2,0,1:T(2,128)(2,1)}), bf16[2,32,2,2048]{3,2,0,1:T(2,128)(2,1)S(1)}, u32[]{:S(2)}, u32[]{:S(2)}) %all-to-all-start.2) | async-done | bytes 524320 | tf_op jit(solution)/shard_map/all_to_all | solution.py:104
  276.6 1.6 gather_fusion.1
  278.2 0.6 fusion.1
  278.8 21.2 %all_to_all.21 = bf16[2,32,2,2048]{3,2,0,1:T(2,128)(2,1)S(1)} all-to-all(bf16[2,32,2,2048]{3,2,0,1:T(2,128)(2,1)S(1)} %fusion.1), channel_id=1, replica_groups=mesh['dp'=32,'seq'=8] {'dp'}, dimensions={1} | all-to-all | bytes 1048576 | tf_op jit(solution)/shard_map/all_to_all | solution.py:108
  300.0 0.4 fusion.4
  300.4 0.8 broadcast_in_dim_squeeze.6
  301.2 0.8 broadcast_in_dim_squeeze.7
  (5 shorter events, 0.0 us)
Async XLA Ops:
  7.2 15.0 %copy-start.4 = (s32[32]{0:T(128)S(1)}, s32[32]{0:T(128)}, u32[]{:S(2)}) copy-start(s32[32]{0:T(128)} %param.17) | copy-start | bytes 388
  10.9 27.9 %all-to-all-start = ((bf16[2,32,2,2048]{3,2,0,1:T(2,128)(2,1)}), bf16[2,32,2,2048]{3,2,0,1:T(2,128)(2,1)S(1)}, u32[]{:S(2)}, u32[]{:S(2)}) async-start(bf16[2,32,2,2048]{3,2,0,1:T(2,128)(2,1)} %pad_maximum_fusion.1), calls=%async_computation | async-start | bytes 1048576 | tf_op jit(solution)/shard_map/all_to_all | solution.py:92
  22.1 115.5 %all-gather.2.cloned.1.call-start = ((), (), s32[]{:S(2)}) async-start(), calls=%async_computation.5 | async-start | bytes 4718592 | tf_op jit(solution)/shard_map/all_gather | solution.py:96
  41.3 23.3 %copy-start.5 = (s32[32]{0:T(128)S(1)}, s32[32]{0:T(128)}, u32[]{:S(2)}) copy-start(s32[32]{0:T(128)} %param.19) | copy-start | bytes 388
  64.0 184.0 %reduce-scatter.2.cloned.1.call-start = ((), (), s32[]{:S(2)}) async-start(), calls=%async_computation.6 | async-start | bytes 4718592 | tf_op jit(solution)/shard_map/reduce_scatter | solution.py:102
  66.0 74.5 %copy-start = (bf16[1,1,256,2048]{3,2,1,0:T(8,128)(2,1)S(1)}, bf16[1,1,256,2048]{3,2,1,0:T(8,128)(2,1)}, u32[]{:S(2)}) copy-start(bf16[1,1,256,2048]{3,2,1,0:T(8,128)(2,1)} %param.11) | copy-start | bytes 3145732
  66.0 74.5 %copy-start.1 = (bf16[1,1,256,2048]{3,2,1,0:T(8,128)(2,1)S(1)}, bf16[1,1,256,2048]{3,2,1,0:T(8,128)(2,1)}, u32[]{:S(2)}) copy-start(bf16[1,1,256,2048]{3,2,1,0:T(8,128)(2,1)} %param.12) | copy-start | bytes 3145732
  66.0 74.5 %copy-start.2 = (bf16[1,1,256,2048]{3,2,1,0:T(8,128)(2,1)S(1)}, bf16[1,1,256,2048]{3,2,1,0:T(8,128)(2,1)}, u32[]{:S(2)}) copy-start(bf16[1,1,256,2048]{3,2,1,0:T(8,128)(2,1)} %param.13) | copy-start | bytes 3145732
  137.6 2.9 copy-start.3
  250.7 25.9 %all-to-all-start.2 = ((bf16[2,32,2,2048]{3,2,0,1:T(2,128)(2,1)}), bf16[2,32,2,2048]{3,2,0,1:T(2,128)(2,1)S(1)}, u32[]{:S(2)}, u32[]{:S(2)}) async-start(bf16[2,32,2,2048]{3,2,0,1:T(2,128)(2,1)} %copy.20), calls=%async_computation.3 | async-start | bytes 1048576 | tf_op jit(solution)/shard_map/all_to_all | solution.py:104
Sparse Core Ops, SparseCore 0:
  64.1 73.4 all-gather.1
  161.0 86.9 reduce-scatter.1

commit v2 on v1

v2 whole, which is shorter than its diff:
```python
import functools

import jax
import jax.numpy as jnp
from jax import lax
from jax.experimental import pallas as pl
from jax.experimental.pallas import tpu as pltpu
from jax.sharding import PartitionSpec as P

HEAD = 128
TILE = 16
CHUNKS = 4
NX = 4
NEG = -1e30
LOG2E = 1.4426950408889634
NT = (((1,), (1,)), ((), ()))
TN = (((0,), (0,)), ((), ()))
NN = (((1,), (0,)), ((), ()))
MESH = pl.DeviceIdType.MESH
BF16 = jnp.bfloat16
F32 = jnp.float32

GATHER_Y_FIRST = ((True, False), (True, False), (True, True), (True, True))
SCATTER_Y_LAST = ((True, False), (True, False), (True, True), (True, True))


PLAN = (
    ("p1", 3), ("p1", 0), ("prep",), ("p2", 3), ("p2", 0), ("p1", 1), ("p1", 2), ("a0", 3), ("au", 3, 0),
    ("ad", 3, 0), ("a0", 0), ("as", 3, 0), ("p2", 1), ("as", 3, 1), ("au", 0, 1), ("ad", 0, 1), ("as", 0, 0),
    ("p2", 2), ("ad", 0, 0), ("au", 0, 0), ("aou", 3, 0), ("aod", 3, 1), ("aou", 3, 1), ("ad", 3, 1), ("au", 3, 1),
    ("af", 0, 1), ("aod", 3, 0), ("aou", 0, 0), ("aod", 0, 0), ("a0", 1), ("a0", 2), ("a3", 3), ("k", 3, 0),
    ("a3", 0), ("k", 0, 0), ("k", 0, 1), ("ad", 1, 0), ("ad", 1, 1), ("as", 2, 0), ("k", 0, 2), ("au", 1, 1),
    ("k", 0, 3), ("as", 1, 0), ("r0", 0, 0), ("as", 2, 1), ("r0", 0, 1), ("au", 2, 0), ("k", 3, 1), ("k", 3, 2),
    ("aod", 1, 0), ("aou", 1, 0), ("au", 1, 0), ("k", 3, 3), ("r0", 3, 0), ("r0", 3, 1), ("aod", 2, 0),
    ("rn", 0, 0, 1, 0), ("rn", 0, 0, 0, 0), ("rn", 0, 0, 1, 1), ("aou", 2, 0), ("af", 1, 1), ("ad", 2, 1),
    ("rr", 0, 1), ("a3", 1), ("k", 1, 0), ("au", 2, 1), ("ad", 2, 0), ("rn", 3, 1, 1, 1), ("k", 1, 1), ("k", 1, 2),
    ("rt", 0, 0), ("k", 1, 3), ("r0", 1, 1), ("aou", 2, 1), ("aod", 2, 1), ("rn", 3, 0, 1, 0), ("rn", 3, 0, 1, 1),
    ("rn", 0, 1, 0, 0), ("rn", 3, 1, 1, 0), ("rn", 3, 0, 0, 0), ("rn", 0, 0, 0, 1), ("rn", 3, 1, 0, 0),
    ("rn", 0, 1, 0, 1), ("rn", 3, 0, 0, 1), ("a3", 2), ("k", 2, 0), ("k", 2, 1), ("k", 2, 2), ("rn", 3, 1, 0, 1),
    ("rt", 3, 0), ("k", 2, 3), ("r0", 2, 1), ("rt", 3, 1), ("r0", 2, 0), ("rf", 0, 1), ("rf", 0, 0), ("p3", 0),
    ("rr", 1, 1), ("rn", 2, 1, 1, 0), ("rf", 3, 0), ("r0", 1, 0), ("rf", 3, 1), ("rn", 2, 1, 1, 1), ("p3", 3),
    ("rn", 2, 0, 1, 0), ("rn", 2, 0, 0, 0), ("rn", 2, 0, 1, 1), ("rn", 1, 0, 1, 1), ("p4", 0), ("rn", 2, 0, 0, 1),
    ("rn", 2, 1, 0, 1), ("rt", 2, 1), ("rn", 1, 0, 1, 0), ("rn", 2, 1, 0, 0), ("rn", 1, 0, 0, 1),
    ("rn", 1, 0, 0, 0), ("rt", 2, 0), ("p4", 3), ("rt", 1, 0), ("rn", 1, 1, 0, 1), ("rn", 1, 1, 0, 0), ("rf", 2, 0),
    ("rf", 2, 1), ("p3", 2), ("rf", 1, 1), ("rf", 1, 0), ("p3", 1), ("p4", 2), ("p4", 1), ("end", 2), ("end", 3),
    ("end", 0), ("end", 1),
)


def dot(a, b, dims):
    return lax.dot_general(a, b, dims, preferred_element_type=F32)


def head_grads(q, g, kp, ko, vp, vo, bias_p, bias_o, scale):
    c = scale * LOG2E
    sp = dot(kp, q, NT) * c + bias_p
    so = dot(ko, q, NT) * c + bias_o
    top = jnp.maximum(jnp.max(sp, 0, keepdims=True), jnp.max(so, 0, keepdims=True))
    pp = jnp.exp2(sp - top)
    po = jnp.exp2(so - top)
    inv = 1.0 / (jnp.sum(pp, 0, keepdims=True) + jnp.sum(po, 0, keepdims=True))
    dp = dot(vp, g, NT)
    do = dot(vo, g, NT)
    delta = (jnp.sum(pp * dp, 0, keepdims=True) + jnp.sum(po * do, 0, keepdims=True)) * inv
    pp = pp * inv
    po = po * inv
    lp = pp.astype(BF16)
    lo = po.astype(BF16)
    tp = (pp * (dp - delta)).astype(BF16)
    to = (po * (do - delta)).astype(BF16)
    gq = (dot(tp, kp, TN) + dot(to, ko, TN)) * scale
    gko = dot(to, q, NN) * scale
    gvo = dot(lo, g, NN)
    gkp = dot(tp, q, NN) * scale
    gvp = dot(lp, g, NN)
    return tuple(x.astype(BF16) for x in (gq, gko, gvo, gkp, gvp))


class Copies:
    def __init__(self, send, recv):
        self.send, self.recv, self.held = send, recv, {}

    def start(self, name, src, dst, target):
        i = len(self.held)
        copy = pltpu.make_async_remote_copy(
            src_ref=src, dst_ref=dst, send_sem=self.send.at[i], recv_sem=self.recv.at[i],
            device_id=target, device_id_type=MESH,
        )
        copy.start()
        self.held[name] = copy

    def arrived(self, name):
        self.held[name].wait_recv()

    def finish(self):
        for copy in self.held.values():
            copy.wait_send()


def kernel(
    count, heads,
    q_in, k_in, v_in, g_in, pk_in, pv_in, group, used_in, len_in,
    gq_out, gk_out, gv_out, pk_out, pv_out,
    q, k, v, g, gq, gk, gv, pin, pout, chosen, gat, part, half_in, full_in, row_in, side_in,
    fin, ordered, bias, inverse,
    load_sem, store_sem, dp_send, dp_recv, seq_send, seq_recv, *held,
):
    stage, back = held[:CHUNKS], held[CHUNKS:]
    rows = q.shape[0]
    shard = pin.shape[1]
    plen = gat.shape[3]
    scale = HEAD**-0.5
    blocks = shard // TILE
    dp = lax.axis_index("dp")
    seq = lax.axis_index("seq")
    yh, x = seq // NX, seq % NX
    x_up, x_down, x_far = (x + 1) % NX, (x + NX - 1) % NX, (x + 2) % NX
    up = (dp, yh * NX + x_up)
    down = (dp, yh * NX + x_down)
    side = (dp, (1 - yh) * NX + x)
    copies = Copies(seq_send, seq_recv)

    def shard_rows(y, xx):
        return pl.ds(pl.multiple_of((y * NX + xx) * shard, shard), shard)

    def place(j):
        return j // (heads * blocks), (j // blocks) % heads, pl.multiple_of((j % blocks) * TILE, TILE)

    def in_shard(ref, c, j):
        kv, h, r = place(j)
        cols = pl.multiple_of((c * heads + h) * HEAD, HEAD)
        return ref.at[kv, pl.ds(r, TILE), pl.ds(cols, HEAD)]

    def spread(phase, c, src, dst):
        def one(k, carry):
            j = (dp + count // 2 + (1 - 2 * (k % 2)) * ((k + 1) // 2)) % count
            pltpu.make_async_remote_copy(
                src_ref=src(j), dst_ref=dst, send_sem=dp_send.at[phase, c],
                recv_sem=dp_recv.at[phase, c], device_id=(j, seq), device_id_type=MESH,
            ).start()
            return carry

        begun.append((phase, c))
        lax.fori_loop(0, count - 1, one, 0)

    begun = []

    def all_of(phase, c, sems):
        some = chosen.at[c, pl.ds(0, count - 1)]
        pltpu.make_async_copy(some, some, sems.at[phase, c]).wait()

    mine = place(dp)

    def p1(c):
        spread(0, c, lambda j: in_shard(pin, c, j), stage[c].at[dp])

    def p2(c):
        stage[c][dp] = in_shard(pin, c, dp)[...]
        all_of(0, c, dp_recv)

        def pick(b, carry):
            chosen[c, b] = stage[c][group[b]]
            return carry

        lax.fori_loop(0, count, pick, 0)
        kv, h, r = mine
        dst = gat.at[c, kv, h, pl.ds(pl.multiple_of(seq * shard + r, TILE), TILE)]
        spread(1, c, lambda j: chosen.at[c, j], dst)
        dst[...] = chosen[c, dp]

    def a0(c):
        all_of(1, c, dp_recv)
        for u in (0, 1):
            own = gat.at[c, u, :, shard_rows(yh, x)]
            for name, to in (("side", side), ("up", up), ("down", down)):
                copies.start(("a", c, u, name), own, own, to)

    def relay_up(c, u, name, y):
        piece = gat.at[c, u, pl.ds(0, heads // 2), shard_rows(y, x_down)]
        copies.start(("a", c, u, name), piece, piece, up)

    def relay_down(c, u, name, y):
        piece = gat.at[c, u, pl.ds(heads // 2, heads // 2), shard_rows(y, x_up)]
        copies.start(("a", c, u, name), piece, piece, down)

    def to_side(c, u, name, xx):
        piece = gat.at[c, u, :, shard_rows(yh, xx)]
        copies.start(("a", c, u, name), piece, piece, side)

    def au(c, u):
        copies.arrived(("a", c, u, "up"))
        relay_up(c, u, "up2", yh)
        if not GATHER_Y_FIRST[c][u]:
            to_side(c, u, "sup", x_down)

    def ad(c, u):
        copies.arrived(("a", c, u, "down"))
        relay_down(c, u, "down2", yh)
        if not GATHER_Y_FIRST[c][u]:
            to_side(c, u, "sdn", x_up)

    def across(c, u):
        copies.arrived(("a", c, u, "side"))
        other = gat.at[c, u, :, shard_rows(1 - yh, x)]
        copies.start(("a", c, u, "oup"), other, other, up)
        copies.start(("a", c, u, "odn"), other, other, down)

    def aou(c, u):
        copies.arrived(("a", c, u, "oup"))
        relay_up(c, u, "oup2", 1 - yh)

    def aod(c, u):
        copies.arrived(("a", c, u, "odn"))
        relay_down(c, u, "odn2", 1 - yh)

    def af(c, u):
        copies.arrived(("a", c, u, "up2"))
        copies.arrived(("a", c, u, "down2"))
        to_side(c, u, "sfar", x_far)

    def a3(c):
        for u in (0, 1):
            if GATHER_Y_FIRST[c][u]:
                names = ("up2", "down2", "oup2", "odn2")
            else:
                names = ("side", "sup", "sdn", "sfar")
            for name in names:
                copies.arrived(("a", c, u, name))

    def compute(c, h):
        cols = pl.ds((c * heads + h) * HEAD, HEAD)
        gq[:, cols], gk[:, cols], gv[:, cols], part[c, 0, h], part[c, 1, h] = head_grads(
            q[:, cols], g[:, cols], gat[c, 0, h], k[:, cols], gat[c, 1, h], v[:, cols],
            bias[:plen], bias[plen:], scale,
        )
        if h == heads - 1:
            store(c)

    def add(dst, src):
        dst[...] = (dst[...].astype(F32) + src[...].astype(F32)).astype(BF16)

    def far_halves(c, u, r, y):
        for d, lo, to in ((0, 0, down), (1, heads // 2, up)):
            copies.start(
                ("r", c, u, r, "half", d),
                part.at[c, u, pl.ds(lo, heads // 2), shard_rows(y, x_far)], half_in.at[c, u, r, d], to,
            )

    def row_of(r):
        return yh if r == 0 else 1 - yh

    def r0(c, u):
        if SCATTER_Y_LAST[c][u]:
            for r in (1, 0):
                far_halves(c, u, r, row_of(r))
        else:
            src = part.at[c, u, :, pl.ds(pl.multiple_of((1 - yh) * NX * shard, shard), NX * shard)]
            copies.start(("r", c, u, "row"), src, row_in.at[c, u], side)

    def rr(c, u):
        copies.arrived(("r", c, u, "row"))
        for xx in (x_far, x_down, x_up, x):
            src = row_in.at[c, u, :, pl.ds(pl.multiple_of(xx * shard, shard), shard)]
            add(part.at[c, u, :, shard_rows(yh, xx)], src)
            if xx is x_far:
                far_halves(c, u, 0, yh)

    def rn(c, u, r, d):
        lo, xx, to = ((0, x_down, down), (heads // 2, x_up, up))[d]
        copies.arrived(("r", c, u, r, "half", d))
        add(part.at[c, u, pl.ds(lo, heads // 2), shard_rows(row_of(r), xx)], half_in.at[c, u, r, d])
        src = part.at[c, u, :, shard_rows(row_of(r), xx)]
        copies.start(("r", c, u, r, "full", d), src, full_in.at[c, u, r, d], to)

    def total(c, u, r):
        for d in (0, 1):
            copies.arrived(("r", c, u, r, "full", d))
        own = part[c, u, :, shard_rows(row_of(r), x)].astype(F32)
        return own + full_in[c, u, r, 0].astype(F32) + full_in[c, u, r, 1].astype(F32)

    def rt(c, u):
        sent = part.at[c, u, :, shard_rows(1 - yh, x)]
        sent[...] = total(c, u, 1).astype(BF16)
        copies.start(("r", c, u, "side"), sent, side_in.at[c, u], side)

    def rf(c, u):
        value = total(c, u, 0)
        if SCATTER_Y_LAST[c][u]:
            copies.arrived(("r", c, u, "side"))
            value = value + side_in[c, u].astype(F32)
        n = heads * blocks
        fin[c, u * n : (u + 1) * n] = value.astype(BF16).reshape(n, TILE, HEAD)

    def p3(c):
        back[c][dp] = fin[c, dp]
        spread(2, c, lambda j: fin.at[c, j], back[c].at[dp])

    def p4(c):
        all_of(2, c, dp_recv)

        def pick(p, carry):
            ordered[c, p] = back[c][inverse[p]]
            return carry

        lax.fori_loop(0, count, pick, 0)
        dst = in_shard(pout, c, dp)
        dst[...] = ordered[c, dp]
        spread(3, c, lambda j: ordered.at[c, j], dst)

    loads = [
        pltpu.make_async_copy(a, b, load_sem.at[i])
        for i, (a, b) in enumerate(
            ((pk_in, pin.at[0]), (pv_in, pin.at[1]), (q_in, q), (k_in, k), (v_in, v), (g_in, g))
        )
    ]
    for copy in loads:
        copy.start()
    barrier = pltpu.get_barrier_semaphore()

    def greet(i, carry):
        pl.semaphore_signal(barrier, inc=1, device_id=((dp + i) % count, seq), device_id_type=MESH)
        return carry

    lax.fori_loop(1, count, greet, 0)
    for target in (up, down, side):
        pl.semaphore_signal(barrier, inc=1, device_id=target, device_id_type=MESH)
    pl.semaphore_wait(barrier, count - 1 + 3)
    loads[0].wait()
    loads[1].wait()

    def prepare():
        length = len_in[0]
        used = used_in[group[dp]]
        bias[:plen] = jnp.where(lax.broadcasted_iota(jnp.int32, (plen, rows), 0) < used, 0.0, NEG)
        key = lax.broadcasted_iota(jnp.int32, (rows, rows), 0)
        query = lax.broadcasted_iota(jnp.int32, (rows, rows), 1)
        bias[plen:] = jnp.where((key <= query) & (key < length), 0.0, NEG)

        def invert(p, carry):
            found = jnp.int32(0)
            for b in range(count):
                found = jnp.where(group[b] == p, b, found)
            inverse[p] = found
            return carry

        lax.fori_loop(0, count, invert, 0)
        for copy in loads[2:]:
            copy.wait()
        for i in range(0, g.shape[1], 512):
            live = lax.broadcasted_iota(jnp.int32, (rows, 512), 0) < length
            g[:, i : i + 512] = jnp.where(live, g[:, i : i + 512], jnp.zeros((rows, 512), BF16))

    stores = []

    def end(c):
        all_of(3, c, dp_recv)

    def store(c):
        cols = pl.ds(c * heads * HEAD, heads * HEAD)
        for i, (a, b) in enumerate(((gq, gq_out), (gk, gk_out), (gv, gv_out))):
            copy = pltpu.make_async_copy(a.at[:, cols], b.at[:, cols], store_sem.at[c, i])
            copy.start()
            stores.append(copy)

    steps = {
        "prep": prepare, "p1": p1, "p2": p2, "a0": a0, "au": au, "ad": ad, "as": across, "aou": aou, "aod": aod,
        "af": af, "a3": a3, "k": compute, "r0": r0, "rr": rr, "rn": rn, "rt": rt, "rf": rf, "p3": p3, "p4": p4,
        "end": end,
    }
    for name, *args in PLAN:
        steps[name](*args)
    for i, out in enumerate((pk_out, pv_out)):
        copy = pltpu.make_async_copy(pout.at[i], out, load_sem.at[i])
        copy.start()
        stores.append(copy)
    for phase, c in begun:
        all_of(phase, c, dp_send)
    copies.finish()
    for copy in stores:
        copy.wait()


def hand_on(*refs):
    ins, outs, held, sem = refs[:5], refs[5:10], refs[10:15], refs[15]
    loads = [pltpu.make_async_copy(a, b, sem.at[0, i]) for i, (a, b) in enumerate(zip(ins, held))]
    stores = [pltpu.make_async_copy(a, b, sem.at[1, i]) for i, (a, b) in enumerate(zip(held, outs))]
    for copy in loads:
        copy.start()
    for load, copy in zip(loads, stores):
        load.wait()
        copy.start()
    for copy in stores:
        copy.wait()


def on_device(resp_q, resp_k, resp_v, resp_grad, prompt_k, prompt_v, group, resp_len, prompt_used):
    rows, width = resp_q.shape[2:]
    shard = prompt_k.shape[2]
    count = lax.axis_size("dp")
    plen = shard * lax.axis_size("seq")
    heads = width // HEAD // CHUNKS
    wide = pltpu.VMEM((rows, width), BF16)
    prompt = pltpu.VMEM((2, shard, width), BF16)
    pieces = pltpu.VMEM((CHUNKS, count, TILE, HEAD), BF16)
    whole = pltpu.VMEM((CHUNKS, 2, heads, plen, HEAD), BF16)
    shape = lambda r: jax.ShapeDtypeStruct((r, width), BF16)
    hbm = pl.BlockSpec(memory_space=pl.ANY)
    scalar = pl.BlockSpec(memory_space=pltpu.SMEM)
    many = 18 * 2 * CHUNKS
    outs = pl.pallas_call(
        functools.partial(kernel, count, heads),
        in_specs=[hbm] * 6 + [scalar] * 3,
        out_specs=[hbm] * 5,
        out_shape=[shape(rows)] * 3 + [shape(shard)] * 2,
        scratch_shapes=[wide] * 7 + [prompt] * 2 + [pieces] + [whole] * 2 + [
            pltpu.VMEM((CHUNKS, 2, 2, 2, heads // 2, shard, HEAD), BF16),
            pltpu.VMEM((CHUNKS, 2, 2, 2, heads, shard, HEAD), BF16),
            pltpu.VMEM((CHUNKS, 2, heads, NX * shard, HEAD), BF16),
            pltpu.VMEM((CHUNKS, 2, heads, shard, HEAD), BF16),
        ] + [pieces] * 2 + [
            pltpu.VMEM((plen + rows, rows), F32),
            pltpu.SMEM((count,), jnp.int32),
            pltpu.SemaphoreType.DMA((6,)),
            pltpu.SemaphoreType.DMA((CHUNKS, 3)),
            pltpu.SemaphoreType.DMA((4, CHUNKS)),
            pltpu.SemaphoreType.DMA((4, CHUNKS)),
            pltpu.SemaphoreType.DMA((many,)),
            pltpu.SemaphoreType.DMA((many,)),
        ] + [pltpu.VMEM((count, TILE, HEAD), BF16)] * (2 * CHUNKS),
        compiler_params=pltpu.CompilerParams(
            collective_id=0, has_side_effects=True, vmem_limit_bytes=56 * 2**20
        ),
    )(
        resp_q[0, 0], resp_k[0, 0], resp_v[0, 0], resp_grad[0, 0], prompt_k[0, 0], prompt_v[0, 0],
        group, prompt_used, resp_len[0],
    )
    buffers = [pltpu.VMEM(a.shape, BF16) for a in outs]
    outs = pl.pallas_call(
        hand_on,
        in_specs=[hbm] * 5,
        out_specs=[hbm] * 5,
        out_shape=[shape(rows)] * 3 + [shape(shard)] * 2,
        scratch_shapes=buffers + [pltpu.SemaphoreType.DMA((2, 5))],
        compiler_params=pltpu.CompilerParams(vmem_limit_bytes=56 * 2**20),
    )(*outs)
    return tuple(a[None, None] for a in outs)


def solution(mesh):
    split = P("dp", "seq", None, None)
    return jax.shard_map(
        on_device,
        mesh=mesh,
        in_specs=(split,) * 6 + (P(), P("dp", "seq"), P()),
        out_specs=(split,) * 5,
        check_vma=False,
    )
```

time: 309 us -> 112 us (0.36)
  waiting for transfers between devices: 191 us -> 0 us
  Pallas kernels: 18.1 us -> 110 us
  blocking collectives: 42.5 us -> 0 us
  starting transfers between devices: 20.4 us -> 0 us
  local copies, waits for them, and re-layouts: 14.8 us -> 0 us
  between operations: 14.8 us -> 1.45 us
  other arithmetic: 6.97 us -> 0 us
    pallas_call x1 -> x2, Pallas kernels: 18.1 us -> 110 us  [the longest x1 107 us: on_device(): pl.pallas_call(functools.partial(kernel, count, heads), in_specs=[hbm] *...]
    reduce_scatter x1 -> x0, waiting for transfers between devices: 87.1 us -> none  [on_device(): summed = lax.psum_scatter(buffer, 'seq', scatter_dimension=1, tiled=True)]
    all_gather x1 -> x0, waiting for transfers between devices: 71.6 us -> none  [on_device(): whole = lax.all_gather(shard, 'seq', axis=1, tiled=True)]
    all_to_all x2 -> x0, blocking collectives: 42.5 us -> none  [the longest x1 21.2 us: on_device(): lax.all_to_all(outgoing, 'dp', split_axis=1, concat_axis=1, tiled=True)]
    all_to_all x2 -> x0, waiting for transfers between devices: 32.6 us -> none  [the longest x1 16.6 us: on_device(): lax.all_to_all(returned, 'dp', split_axis=1, concat_axis=1, tiled=True)]
    all_to_all x2 -> x0, starting transfers between devices: 20.3 us -> none  [the longest x1 11.1 us: on_device(): lax.all_to_all(stacked, 'dp', split_axis=1, concat_axis=1, tiled=True)]
    another operation x4 -> x0, local copies, waits for them, and re-layouts: 3.88 us -> none  [the longest x2 2.27 us: on_device(): jnp.stack([prompt_k[0, 0], prompt_v[0, 0]], axis=0)]
    another operation x2 -> x0, other arithmetic: 3.78 us -> none  [the longest x1 2.3 us: on_device(): buffer = jnp.stack([part_k, part_v], axis=0)]
  transfers between devices with their start and end apart: 4 -> 0, of which waited for: 4 -> 0; matrix products, arithmetic and copies ran while one was open for 1% -> 0% of each run, Pallas kernels for 0% -> 0%
where the time goes in v2:
time: 112 us
  Pallas kernels  110 us (98%)
  between operations  1.45 us (1%)
    pallas_call x1, Pallas kernels, on_device(): pl.pallas_call(functools.partial(kernel, count, heads), in_specs=[hbm] *...  107 us
    pallas_call x1, Pallas kernels, on_device(): pl.pallas_call(hand_on, in_specs=[hbm] * 5, out_specs=[hbm] * 5, out_shap...  3.14 us

profile of v2, /device:TPU:1, one launch (start us, length us, event | category | flops | bytes accessed | tf_op | source)
XLA Modules:
  0.0 111.5 jit_solution(948298410844884844)
XLA Ops:
  1.3 107.0 %shard_map.128 = (bf16[256,2048]{1,0:T(8,128)(2,1)}, bf16[256,2048]{1,0:T(8,128)(2,1)}, bf16[256,2048]{1,0:T(8,128)(2,1)}, bf16[64,2048]{1,0:T(8,128)(2,1)}, bf16[64,2048]{1,0:T(8,128)(2,1)}) custom-call(bf16[256,2048]{1,0:T(8,128)(2,1)} %bitcast.13, bf16[256,2048]{1,0:T(8,128)(2,1)} %bitcast.14, bf16[256,2048]{1,0:T(8,128)(2,1)} %bitcast.15, ...), custom_call_target="tpu_custom_call" | custom-call | tf_op jit(solution)/shard_map/pallas_call | solution.py:410
  108.2 3.1 %shard_map.129 = (bf16[256,2048]{1,0:T(8,128)(2,1)}, bf16[256,2048]{1,0:T(8,128)(2,1)}, bf16[256,2048]{1,0:T(8,128)(2,1)}, bf16[64,2048]{1,0:T(8,128)(2,1)}, bf16[64,2048]{1,0:T(8,128)(2,1)}) custom-call(bf16[256,2048]{1,0:T(8,128)(2,1)} %get-tuple-element.15.refs_0_, bf16[256,2048]{1,0:T(8,128)(2,1)} %get-tuple-element.16.refs_1_, ...), custom_call_target="tpu_custom_call" | custom-call | tf_op jit(solution)/shard_map/pallas_call | solution.py:438

commit v3 on v2

--- a/solution.py
+++ b/solution.py
@@ -25,25 +25,24 @@
 
 
 PLAN = (
-    ("p1", 3), ("p1", 0), ("prep",), ("p2", 3), ("p2", 0), ("p1", 1), ("p1", 2), ("a0", 3), ("au", 3, 0),
-    ("ad", 3, 0), ("a0", 0), ("as", 3, 0), ("p2", 1), ("as", 3, 1), ("au", 0, 1), ("ad", 0, 1), ("as", 0, 0),
-    ("p2", 2), ("ad", 0, 0), ("au", 0, 0), ("aou", 3, 0), ("aod", 3, 1), ("aou", 3, 1), ("ad", 3, 1), ("au", 3, 1),
-    ("af", 0, 1), ("aod", 3, 0), ("aou", 0, 0), ("aod", 0, 0), ("a0", 1), ("a0", 2), ("a3", 3), ("k", 3, 0),
-    ("a3", 0), ("k", 0, 0), ("k", 0, 1), ("ad", 1, 0), ("ad", 1, 1), ("as", 2, 0), ("k", 0, 2), ("au", 1, 1),
-    ("k", 0, 3), ("as", 1, 0), ("r0", 0, 0), ("as", 2, 1), ("r0", 0, 1), ("au", 2, 0), ("k", 3, 1), ("k", 3, 2),
-    ("aod", 1, 0), ("aou", 1, 0), ("au", 1, 0), ("k", 3, 3), ("r0", 3, 0), ("r0", 3, 1), ("aod", 2, 0),
-    ("rn", 0, 0, 1, 0), ("rn", 0, 0, 0, 0), ("rn", 0, 0, 1, 1), ("aou", 2, 0), ("af", 1, 1), ("ad", 2, 1),
-    ("rr", 0, 1), ("a3", 1), ("k", 1, 0), ("au", 2, 1), ("ad", 2, 0), ("rn", 3, 1, 1, 1), ("k", 1, 1), ("k", 1, 2),
-    ("rt", 0, 0), ("k", 1, 3), ("r0", 1, 1), ("aou", 2, 1), ("aod", 2, 1), ("rn", 3, 0, 1, 0), ("rn", 3, 0, 1, 1),
-    ("rn", 0, 1, 0, 0), ("rn", 3, 1, 1, 0), ("rn", 3, 0, 0, 0), ("rn", 0, 0, 0, 1), ("rn", 3, 1, 0, 0),
-    ("rn", 0, 1, 0, 1), ("rn", 3, 0, 0, 1), ("a3", 2), ("k", 2, 0), ("k", 2, 1), ("k", 2, 2), ("rn", 3, 1, 0, 1),
-    ("rt", 3, 0), ("k", 2, 3), ("r0", 2, 1), ("rt", 3, 1), ("r0", 2, 0), ("rf", 0, 1), ("rf", 0, 0), ("p3", 0),
-    ("rr", 1, 1), ("rn", 2, 1, 1, 0), ("rf", 3, 0), ("r0", 1, 0), ("rf", 3, 1), ("rn", 2, 1, 1, 1), ("p3", 3),
-    ("rn", 2, 0, 1, 0), ("rn", 2, 0, 0, 0), ("rn", 2, 0, 1, 1), ("rn", 1, 0, 1, 1), ("p4", 0), ("rn", 2, 0, 0, 1),
-    ("rn", 2, 1, 0, 1), ("rt", 2, 1), ("rn", 1, 0, 1, 0), ("rn", 2, 1, 0, 0), ("rn", 1, 0, 0, 1),
-    ("rn", 1, 0, 0, 0), ("rt", 2, 0), ("p4", 3), ("rt", 1, 0), ("rn", 1, 1, 0, 1), ("rn", 1, 1, 0, 0), ("rf", 2, 0),
-    ("rf", 2, 1), ("p3", 2), ("rf", 1, 1), ("rf", 1, 0), ("p3", 1), ("p4", 2), ("p4", 1), ("end", 2), ("end", 3),
-    ("end", 0), ("end", 1),
+    ("p1", 2), ("p1", 0), ("prep",), ("p2", 2), ("p2", 0), ("p1", 1), ("a0", 2), ("p1", 3), ("a0", 0), ("as", 2, 0),
+    ("as", 2, 1), ("au", 2, 0), ("p2", 1), ("ad", 0, 1), ("as", 0, 0), ("au", 0, 1), ("p2", 3), ("aou", 2, 0),
+    ("aod", 2, 0), ("aou", 2, 1), ("ad", 2, 1), ("au", 2, 1), ("ad", 2, 0), ("aod", 2, 1), ("a0", 1), ("af", 0, 1),
+    ("aod", 0, 0), ("au", 0, 0), ("aou", 0, 0), ("ad", 0, 0), ("a0", 3), ("a3", 2), ("k", 2, 0), ("k", 2, 1),
+    ("k", 2, 2), ("as", 1, 0), ("au", 1, 1), ("ad", 1, 1), ("ad", 1, 0), ("a3", 0), ("k", 2, 3), ("r0", 2, 0),
+    ("au", 1, 0), ("r0", 2, 1), ("k", 0, 0), ("k", 0, 1), ("k", 0, 2), ("af", 1, 1), ("aou", 1, 0), ("aod", 1, 0),
+    ("as", 3, 1), ("k", 0, 3), ("r0", 0, 1), ("as", 3, 0), ("rn", 2, 0, 1, 1), ("rn", 2, 0, 1, 0), ("r0", 0, 0),
+    ("rn", 2, 1, 1, 1), ("rn", 2, 1, 1, 0), ("a3", 1), ("k", 1, 0), ("k", 1, 1), ("k", 1, 2), ("au", 3, 0),
+    ("aou", 3, 0), ("aou", 3, 1), ("aod", 3, 1), ("au", 3, 1), ("aod", 3, 0), ("ad", 3, 0), ("rt", 2, 0),
+    ("ad", 3, 1), ("k", 1, 3), ("r0", 1, 1), ("rn", 2, 1, 0, 1), ("rn", 0, 0, 1, 0), ("rn", 2, 1, 0, 0),
+    ("rr", 0, 1), ("rn", 2, 0, 0, 0), ("rn", 0, 0, 1, 1), ("rt", 2, 1), ("rn", 2, 0, 0, 1), ("rn", 0, 0, 0, 0),
+    ("rn", 0, 0, 0, 1), ("a3", 3), ("k", 3, 0), ("k", 3, 1), ("k", 3, 2), ("k", 3, 3), ("r0", 3, 0), ("rt", 0, 0),
+    ("rn", 0, 1, 0, 1), ("rn", 0, 1, 0, 0), ("rf", 2, 0), ("r0", 3, 1), ("rf", 2, 1), ("p3", 2), ("rn", 3, 0, 1, 1),
+    ("rn", 3, 0, 1, 0), ("r0", 1, 0), ("rf", 0, 0), ("rf", 0, 1), ("p3", 0), ("rn", 3, 1, 1, 0), ("rn", 3, 1, 1, 1),
+    ("rr", 1, 1), ("rt", 3, 0), ("rn", 1, 0, 1, 1), ("rn", 1, 0, 1, 0), ("rn", 3, 0, 0, 1), ("p4", 2),
+    ("rn", 3, 0, 0, 0), ("rn", 3, 1, 0, 1), ("rt", 3, 1), ("rn", 1, 0, 0, 1), ("rn", 3, 1, 0, 0), ("p4", 0),
+    ("rn", 1, 0, 0, 0), ("rt", 1, 0), ("rn", 1, 1, 0, 0), ("rf", 3, 0), ("rn", 1, 1, 0, 1), ("rf", 3, 1), ("p3", 3),
+    ("rf", 1, 0), ("rf", 1, 1), ("p3", 1), ("end", 0), ("p4", 3), ("end", 2), ("p4", 1), ("end", 3), ("end", 1),
 )
 
 
@@ -100,10 +99,10 @@
 def kernel(
     count, heads,
     q_in, k_in, v_in, g_in, pk_in, pv_in, group, used_in, len_in,
-    gq_out, gk_out, gv_out, pk_out, pv_out,
-    q, k, v, g, gq, gk, gv, pin, pout, chosen, gat, part, half_in, full_in, row_in, side_in,
+    gq, gk, gv, pout,
+    q, k, v, g, pin, chosen, gat, part, half_in, full_in, row_in, side_in,
     fin, ordered, bias, inverse,
-    load_sem, store_sem, dp_send, dp_recv, seq_send, seq_recv, *held,
+    load_sem, dp_send, dp_recv, seq_send, seq_recv, *held,
 ):
     stage, back = held[:CHUNKS], held[CHUNKS:]
     rows = q.shape[0]
@@ -124,7 +123,8 @@
         return pl.ds(pl.multiple_of((y * NX + xx) * shard, shard), shard)
 
     def place(j):
-        return j // (heads * blocks), (j // blocks) % heads, pl.multiple_of((j % blocks) * TILE, TILE)
+        h = lax.rem(lax.div(j, blocks), heads)
+        return lax.div(j, heads * blocks), h, pl.multiple_of(lax.rem(j, blocks) * TILE, TILE)
 
     def in_shard(ref, c, j):
         kv, h, r = place(j)
@@ -133,7 +133,9 @@
 
     def spread(phase, c, src, dst):
         def one(k, carry):
-            j = (dp + count // 2 + (1 - 2 * (k % 2)) * ((k + 1) // 2)) % count
+            step = lax.div(k + 1, 2)
+            j = dp + count // 2 + jnp.where(lax.rem(k, 2) == 0, step, -step)
+            j = jnp.where(j >= count, j - count, j)
             pltpu.make_async_remote_copy(
                 src_ref=src(j), dst_ref=dst, send_sem=dp_send.at[phase, c],
                 recv_sem=dp_recv.at[phase, c], device_id=(j, seq), device_id_type=MESH,
@@ -233,8 +235,6 @@
             q[:, cols], g[:, cols], gat[c, 0, h], k[:, cols], gat[c, 1, h], v[:, cols],
             bias[:plen], bias[plen:], scale,
         )
-        if h == heads - 1:
-            store(c)
 
     def add(dst, src):
         dst[...] = (dst[...].astype(F32) + src[...].astype(F32)).astype(BF16)
@@ -329,7 +329,7 @@
     loads[1].wait()
 
     def prepare():
-        length = len_in[0]
+        length = len_in[0, 0]
         used = used_in[group[dp]]
         bias[:plen] = jnp.where(lax.broadcasted_iota(jnp.int32, (plen, rows), 0) < used, 0.0, NEG)
         key = lax.broadcasted_iota(jnp.int32, (rows, rows), 0)
@@ -350,17 +350,8 @@
             live = lax.broadcasted_iota(jnp.int32, (rows, 512), 0) < length
             g[:, i : i + 512] = jnp.where(live, g[:, i : i + 512], jnp.zeros((rows, 512), BF16))
 
-    stores = []
-
     def end(c):
         all_of(3, c, dp_recv)
-
-    def store(c):
-        cols = pl.ds(c * heads * HEAD, heads * HEAD)
-        for i, (a, b) in enumerate(((gq, gq_out), (gk, gk_out), (gv, gv_out))):
-            copy = pltpu.make_async_copy(a.at[:, cols], b.at[:, cols], store_sem.at[c, i])
-            copy.start()
-            stores.append(copy)
 
     steps = {
         "prep": prepare, "p1": p1, "p2": p2, "a0": a0, "au": au, "ad": ad, "as": across, "aou": aou, "aod": aod,
@@ -369,27 +360,18 @@
     }
     for name, *args in PLAN:
         steps[name](*args)
-    for i, out in enumerate((pk_out, pv_out)):
-        copy = pltpu.make_async_copy(pout.at[i], out, load_sem.at[i])
-        copy.start()
-        stores.append(copy)
     for phase, c in begun:
         all_of(phase, c, dp_send)
     copies.finish()
-    for copy in stores:
-        copy.wait()
-
-
-def hand_on(*refs):
-    ins, outs, held, sem = refs[:5], refs[5:10], refs[10:15], refs[15]
-    loads = [pltpu.make_async_copy(a, b, sem.at[0, i]) for i, (a, b) in enumerate(zip(ins, held))]
-    stores = [pltpu.make_async_copy(a, b, sem.at[1, i]) for i, (a, b) in enumerate(zip(held, outs))]
-    for copy in loads:
+
+
+def hand_on(gq, gk, gv, gp, *refs):
+    outs, sem = refs[:5], refs[5]
+    ins = (gq, gk, gv, gp.at[0], gp.at[1])
+    copies = [pltpu.make_async_copy(a, b, sem.at[i]) for i, (a, b) in enumerate(zip(ins, outs))]
+    for copy in copies:
         copy.start()
-    for load, copy in zip(loads, stores):
-        load.wait()
-        copy.start()
-    for copy in stores:
+    for copy in copies:
         copy.wait()
 
 
@@ -405,14 +387,15 @@
     whole = pltpu.VMEM((CHUNKS, 2, heads, plen, HEAD), BF16)
     shape = lambda r: jax.ShapeDtypeStruct((r, width), BF16)
     hbm = pl.BlockSpec(memory_space=pl.ANY)
+    vmem = pl.BlockSpec(memory_space=pltpu.VMEM)
     scalar = pl.BlockSpec(memory_space=pltpu.SMEM)
     many = 18 * 2 * CHUNKS
     outs = pl.pallas_call(
         functools.partial(kernel, count, heads),
         in_specs=[hbm] * 6 + [scalar] * 3,
-        out_specs=[hbm] * 5,
-        out_shape=[shape(rows)] * 3 + [shape(shard)] * 2,
-        scratch_shapes=[wide] * 7 + [prompt] * 2 + [pieces] + [whole] * 2 + [
+        out_specs=[vmem] * 4,
+        out_shape=[wide] * 3 + [prompt],
+        scratch_shapes=[wide] * 4 + [prompt] + [pieces] + [whole] * 2 + [
             pltpu.VMEM((CHUNKS, 2, 2, 2, heads // 2, shard, HEAD), BF16),
             pltpu.VMEM((CHUNKS, 2, 2, 2, heads, shard, HEAD), BF16),
             pltpu.VMEM((CHUNKS, 2, heads, NX * shard, HEAD), BF16),
@@ -421,27 +404,25 @@
             pltpu.VMEM((plen + rows, rows), F32),
             pltpu.SMEM((count,), jnp.int32),
             pltpu.SemaphoreType.DMA((6,)),
-            pltpu.SemaphoreType.DMA((CHUNKS, 3)),
             pltpu.SemaphoreType.DMA((4, CHUNKS)),
             pltpu.SemaphoreType.DMA((4, CHUNKS)),
             pltpu.SemaphoreType.DMA((many,)),
             pltpu.SemaphoreType.DMA((many,)),
         ] + [pltpu.VMEM((count, TILE, HEAD), BF16)] * (2 * CHUNKS),
         compiler_params=pltpu.CompilerParams(
-            collective_id=0, has_side_effects=True, vmem_limit_bytes=56 * 2**20
+            collective_id=0, has_side_effects=True, vmem_limit_bytes=58 * 2**20
         ),
     )(
         resp_q[0, 0], resp_k[0, 0], resp_v[0, 0], resp_grad[0, 0], prompt_k[0, 0], prompt_v[0, 0],
-        group, prompt_used, resp_len[0],
+        group, prompt_used, resp_len,
     )
-    buffers = [pltpu.VMEM(a.shape, BF16) for a in outs]
     outs = pl.pallas_call(
         hand_on,
-        in_specs=[hbm] * 5,
+        in_specs=[vmem] * 4,
         out_specs=[hbm] * 5,
         out_shape=[shape(rows)] * 3 + [shape(shard)] * 2,
-        scratch_shapes=buffers + [pltpu.SemaphoreType.DMA((2, 5))],
-        compiler_params=pltpu.CompilerParams(vmem_limit_bytes=56 * 2**20),
+        scratch_shapes=[pltpu.SemaphoreType.DMA((5,))],
+        compiler_params=pltpu.CompilerParams(vmem_limit_bytes=16 * 2**20),
     )(*outs)
     return tuple(a[None, None] for a in outs)
 

time: 112 us -> 108 us (0.964)
  Pallas kernels: 110 us -> 106 us
    pallas_call x1, Pallas kernels: 107 us -> 105 us  [on_device(): pl.pallas_call(functools.partial(kernel, count, heads), in_specs=[hbm] *...]
    pallas_call x1, Pallas kernels: 3.14 us -> 1.87 us  [on_device(): pl.pallas_call(hand_on, in_specs=[vmem] * 4, out_specs=[hbm] * 5, out_sha...]
where the time goes in v3:
time: 108 us
  Pallas kernels  106 us (98%)
  between operations  1.45 us (1%)
    pallas_call x1, Pallas kernels, on_device(): pl.pallas_call(functools.partial(kernel, count, heads), in_specs=[hbm] *...  105 us

profile of v3, /device:TPU:1, one launch (start us, length us, event | category | flops | bytes accessed | tf_op | source)
XLA Modules:
  0.0 107.9 jit_solution(15472174952326271920)
XLA Ops:
  1.3 104.6 %shard_map.128 = (bf16[256,2048]{1,0:T(8,128)(2,1)S(1)}, bf16[256,2048]{1,0:T(8,128)(2,1)S(1)}, bf16[256,2048]{1,0:T(8,128)(2,1)S(1)}, bf16[2,64,2048]{2,1,0:T(8,128)(2,1)S(1)}) custom-call(bf16[256,2048]{1,0:T(8,128)(2,1)} %bitcast.11, bf16[256,2048]{1,0:T(8,128)(2,1)} %bitcast.12, bf16[256,2048]{1,0:T(8,128)(2,1)} %bitcast.13, bf16[256,2048]{1,0:T(8,128)(2,1)} %bitcast.14, ...), custom_call_target="tpu_custom_call" | custom-call | tf_op jit(solution)/shard_map/pallas_call | solution.py:393
  105.9 1.9 %shard_map.129 = (bf16[256,2048]{1,0:T(8,128)(2,1)}, bf16[256,2048]{1,0:T(8,128)(2,1)}, bf16[256,2048]{1,0:T(8,128)(2,1)}, bf16[64,2048]{1,0:T(8,128)(2,1)}, bf16[64,2048]{1,0:T(8,128)(2,1)}) custom-call(bf16[256,2048]{1,0:T(8,128)(2,1)S(1)} %get-tuple-element.14.gq, bf16[256,2048]{1,0:T(8,128)(2,1)S(1)} %get-tuple-element.15.gk, ...), custom_call_target="tpu_custom_call" | custom-call | tf_op jit(solution)/shard_map/pallas_call | solution.py:419

commit v4 on v3

--- a/solution.py
+++ b/solution.py
@@ -42,7 +42,8 @@
     ("rr", 1, 1), ("rt", 3, 0), ("rn", 1, 0, 1, 1), ("rn", 1, 0, 1, 0), ("rn", 3, 0, 0, 1), ("p4", 2),
     ("rn", 3, 0, 0, 0), ("rn", 3, 1, 0, 1), ("rt", 3, 1), ("rn", 1, 0, 0, 1), ("rn", 3, 1, 0, 0), ("p4", 0),
     ("rn", 1, 0, 0, 0), ("rt", 1, 0), ("rn", 1, 1, 0, 0), ("rf", 3, 0), ("rn", 1, 1, 0, 1), ("rf", 3, 1), ("p3", 3),
-    ("rf", 1, 0), ("rf", 1, 1), ("p3", 1), ("end", 0), ("p4", 3), ("end", 2), ("p4", 1), ("end", 3), ("end", 1),
+    ("rf", 1, 0), ("rf", 1, 1), ("p3", 1), ("end", 0), ("p4", 3), ("end", 2), ("p4", 1), ("flush", 2), ("end", 3),
+    ("end", 1),
 )
 
 
@@ -77,7 +78,7 @@
 
 class Copies:
     def __init__(self, send, recv):
-        self.send, self.recv, self.held = send, recv, {}
+        self.send, self.recv, self.held, self.ended = send, recv, {}, set()
 
     def start(self, name, src, dst, target):
         i = len(self.held)
@@ -92,8 +93,9 @@
         self.held[name].wait_recv()
 
     def finish(self):
-        for copy in self.held.values():
-            copy.wait_send()
+        for name in [name for name in self.held if name not in self.ended]:
+            self.held[name].wait_send()
+            self.ended.add(name)
 
 
 def kernel(
@@ -353,16 +355,20 @@
     def end(c):
         all_of(3, c, dp_recv)
 
+    def flush(keep):
+        copies.finish()
+        for phase, c in begun[: len(begun) - keep]:
+            all_of(phase, c, dp_send)
+        del begun[: len(begun) - keep]
+
     steps = {
         "prep": prepare, "p1": p1, "p2": p2, "a0": a0, "au": au, "ad": ad, "as": across, "aou": aou, "aod": aod,
         "af": af, "a3": a3, "k": compute, "r0": r0, "rr": rr, "rn": rn, "rt": rt, "rf": rf, "p3": p3, "p4": p4,
-        "end": end,
+        "end": end, "flush": flush,
     }
     for name, *args in PLAN:
         steps[name](*args)
-    for phase, c in begun:
-        all_of(phase, c, dp_send)
-    copies.finish()
+    flush(0)
 
 
 def hand_on(gq, gk, gv, gp, *refs):

time: 108 us -> 108 us (level)
  no operation moved by 1% of the time
where the time goes in v4:
time: 108 us
  Pallas kernels  106 us (98%)
  between operations  1.45 us (1%)
    pallas_call x1, Pallas kernels, on_device(): pl.pallas_call(functools.partial(kernel, count, heads), in_specs=[hbm] *...  104 us

profile of v4, /device:TPU:1, one launch (start us, length us, event | category | flops | bytes accessed | tf_op | source)
XLA Modules:
  0.0 107.7 jit_solution(1879219666116671193)
XLA Ops:
  1.3 104.4 %shard_map.128 = (bf16[256,2048]{1,0:T(8,128)(2,1)S(1)}, bf16[256,2048]{1,0:T(8,128)(2,1)S(1)}, bf16[256,2048]{1,0:T(8,128)(2,1)S(1)}, bf16[2,64,2048]{2,1,0:T(8,128)(2,1)S(1)}) custom-call(bf16[256,2048]{1,0:T(8,128)(2,1)} %bitcast.11, bf16[256,2048]{1,0:T(8,128)(2,1)} %bitcast.12, bf16[256,2048]{1,0:T(8,128)(2,1)} %bitcast.13, bf16[256,2048]{1,0:T(8,128)(2,1)} %bitcast.14, ...), custom_call_target="tpu_custom_call" | custom-call | tf_op jit(solution)/shard_map/pallas_call | solution.py:399
  105.7 1.9 %shard_map.129 = (bf16[256,2048]{1,0:T(8,128)(2,1)}, bf16[256,2048]{1,0:T(8,128)(2,1)}, bf16[256,2048]{1,0:T(8,128)(2,1)}, bf16[64,2048]{1,0:T(8,128)(2,1)}, bf16[64,2048]{1,0:T(8,128)(2,1)}) custom-call(bf16[256,2048]{1,0:T(8,128)(2,1)S(1)} %get-tuple-element.14.gq, bf16[256,2048]{1,0:T(8,128)(2,1)S(1)} %get-tuple-element.15.gk, ...), custom_call_target="tpu_custom_call" | custom-call | tf_op jit(solution)/shard_map/pallas_call | solution.py:425
